TPU v7x, 1024 devices: a whole 8x8x8 slice. The times are simulated.
1024 devices in a mesh: section: 16 (over y, z_lo), dp: 8 (over z_hi, core), tensor: 8 (over x).
Axes of the slice: x: 8, y: 8, z: 8 (z_hi: 4, z_lo: 2; z = z_hi * 2 + z_lo), core: 2. Of those that a mesh axis runs over, the one named last changes fastest.
Arguments:
- down_hidden: bfloat16 [16, 512, 4096], P('section', 'dp'), may hold values from -6 to 6
- up_hidden: bfloat16 [16, 512, 4096], P('section', 'dp'), may hold values from -6 to 6
- down_cot: bfloat16 [16, 512, 1024], P('section', 'dp', 'tensor'), may hold values from -0.19921875 to 0.19921875
- up_cot: bfloat16 [16, 512, 1024], P('section', 'dp', 'tensor'), may hold values from -0.19921875 to 0.19921875
- down_weight: bfloat16 [16, 4096, 1024], P('section', None, 'tensor'), may hold values from -0.09375 to 0.09375
- up_weight: bfloat16 [16, 4096, 1024], P('section', None, 'tensor'), may hold values from -0.09375 to 0.09375
- master: float32 [16, 2, 4096, 1024], P('section', None, 'dp', 'tensor'), may hold values from -3 to 3
- moment1: float32 [16, 2, 4096, 1024], P('section', None, 'dp', 'tensor'), may hold values from -1.2 to 1.2
- moment2: float32 [16, 2, 4096, 1024], P('section', None, 'dp', 'tensor'), may hold values from 0.01 to 1
Outputs:
- down_values: bfloat16 [16, 512, 1024], P('section', 'dp', 'tensor')
- up_values: bfloat16 [16, 512, 1024], P('section', 'dp', 'tensor')
- new_master: float32 [16, 2, 4096, 1024], P('section', None, 'dp', 'tensor')
- new_moment1: float32 [16, 2, 4096, 1024], P('section', None, 'dp', 'tensor')
- new_moment2: float32 [16, 2, 4096, 1024], P('section', None, 'dp', 'tensor')
All inputs are finite; a program needn't handle non-finite values.
Results may differ from a plain program's by a relative error of at most 0.0075.
Values may be sent and summed in bfloat16 or wider, within the bound.
A program may use at most 32 MiB of HBM per device.

v0:
```python
import jax
import jax.numpy as jnp
from jax import lax
from jax.sharding import PartitionSpec as P

STEP = 20


def passed_along(block, axis, distance):
    devices = range(lax.axis_size(axis))
    route = [((i - distance) % len(devices), i) for i in devices]
    return lax.ppermute(block, axis, route)


def normalize(hidden):
    values = hidden.astype(jnp.float32)
    factor = lax.rsqrt(jnp.mean(values * values, axis=-1, keepdims=True) + 1e-05)
    return (values * factor).astype(jnp.bfloat16)


def contract(features, gradient):
    return lax.dot_general(
        features, gradient, (((0,), (0,)), ((), ())), preferred_element_type=jnp.float32
    )


def shards(
    down_hidden, up_hidden, down_cot, up_cot, down_weight, up_weight, master, moment1, moment2
):
    arrived_down = passed_along(down_hidden, "section", 1)
    arrived_up = passed_along(up_hidden, "section", -1)
    down_normed = normalize(arrived_down[0])
    up_normed = normalize(arrived_up[0])
    down_values = jnp.dot(down_normed, down_weight[0], preferred_element_type=jnp.float32).astype(
        jnp.bfloat16
    )
    up_values = jnp.dot(up_normed, up_weight[0], preferred_element_type=jnp.float32).astype(
        jnp.bfloat16
    )
    partial_down = contract(down_normed, down_cot[0])
    partial_up = contract(up_normed, up_cot[0])
    summed = lax.psum_scatter(
        jnp.stack([partial_down, partial_up]).astype(jnp.bfloat16),
        "dp",
        scatter_dimension=1,
        tiled=True,
    ).astype(jnp.float32)
    section_count = lax.axis_size("section")
    pieces = summed.reshape(2, section_count, -1)
    for turn in range(2):
        pieces = lax.all_to_all(
            pieces.astype(jnp.bfloat16), "section", split_axis=1, concat_axis=1, tiled=True
        ).astype(pieces.dtype)
        if turn == 0:
            pieces = pieces[:, ::-1, :]
    shifted = pieces.reshape(summed.shape)
    totals = (summed + shifted[::-1])[None]
    new_moment1 = 0.9 * moment1 + 0.1 * totals
    new_moment2 = 0.95 * moment2 + 0.05 * totals * totals
    first_fix = 1.0 - 0.9**STEP
    second_fix = 1.0 - 0.95**STEP
    new_master = master - 0.05 * (new_moment1 / first_fix) / (
        jnp.sqrt(new_moment2 / second_fix) + 1e-08
    )
    return (down_values[None], up_values[None], new_master, new_moment1, new_moment2)


def solution(mesh):
    return jax.shard_map(
        shards,
        mesh=mesh,
        in_specs=(
            P("section", "dp", None),
            P("section", "dp", None),
            P("section", "dp", "tensor"),
            P("section", "dp", "tensor"),
            P("section", None, "tensor"),
            P("section", None, "tensor"),
            P("section", None, "dp", "tensor"),
            P("section", None, "dp", "tensor"),
            P("section", None, "dp", "tensor"),
        ),
        out_specs=(
            P("section", "dp", "tensor"),
            P("section", "dp", "tensor"),
            P("section", None, "dp", "tensor"),
            P("section", None, "dp", "tensor"),
            P("section", None, "dp", "tensor"),
        ),
        check_vma=False,
    )
```

profile of v0, /device:TPU:2, one launch (start us, length us, event | category | flops | bytes accessed | tf_op | source)
XLA Modules:
  0.0 145.4 jit_solution(4292656660435614622)
XLA Ops:
  7.2 0.0 copy-start
  7.2 0.0 copy-start.4
  7.2 0.0 reduce-scatter.2.cloned.1.call-start
  7.2 5.3 %collective-permute-start = (bf16[1,64,4096]{2,1,0:T(8,128)(2,1)}, bf16[1,64,4096]{2,1,0:T(8,128)(2,1)S(1)}, u32[]{:S(2)}, u32[]{:S(2)}) collective-permute-start(bf16[1,64,4096]{2,1,0:T(8,128)(2,1)} %param.9), channel_id=1, source_target_pairs={{960,0},{0,64},{64,128},{128,192},{192,256},{256,320},{320,384},{3... | collective-permute-start | bytes 1572872 | tf_op jit(solution)/shard_map/ppermute | solution.py:12
  12.6 5.6 %collective-permute-start.1 = (bf16[1,64,4096]{2,1,0:T(8,128)(2,1)}, bf16[1,64,4096]{2,1,0:T(8,128)(2,1)S(1)}, u32[]{:S(2)}, u32[]{:S(2)}) collective-permute-start(bf16[1,64,4096]{2,1,0:T(8,128)(2,1)} %param.10), channel_id=1, source_target_pairs={{64,0},{128,64},{192,128},{256,192},{320,256},{384,320},{448,384},... | collective-permute-start | bytes 1572872 | tf_op jit(solution)/shard_map/ppermute | solution.py:12
  18.2 17.1 %collective-permute-done = bf16[1,64,4096]{2,1,0:T(8,128)(2,1)S(1)} collective-permute-done((bf16[1,64,4096]{2,1,0:T(8,128)(2,1)}, bf16[1,64,4096]{2,1,0:T(8,128)(2,1)S(1)}, u32[]{:S(2)}, u32[]{:S(2)}) %collective-permute-start) | collective-permute-done | bytes 524320 | tf_op jit(solution)/shard_map/ppermute | solution.py:12
  35.3 0.2 fusion.4
  35.5 3.8 %collective-permute-done.1 = bf16[1,64,4096]{2,1,0:T(8,128)(2,1)S(1)} collective-permute-done((bf16[1,64,4096]{2,1,0:T(8,128)(2,1)}, bf16[1,64,4096]{2,1,0:T(8,128)(2,1)S(1)}, u32[]{:S(2)}, u32[]{:S(2)}) %collective-permute-start.1) | collective-permute-done | bytes 524320 | tf_op jit(solution)/shard_map/ppermute | solution.py:12
  39.3 0.2 fusion.6
  39.5 1.3 fusion
  40.8 0.0 copy-done.4
  40.8 0.6 fusion.1
  41.4 1.5 %pad_maximum_fusion = bf16[2,4096,128]{2,1,0:T(8,128)(2,1)} fusion(bf16[1,4096,128]{2,1,0:T(8,128)(2,1)S(1)} %fusion.1, bf16[1,4096,128]{2,1,0:T(8,128)(2,1)S(1)} %fusion), kind=kLoop, calls=%fused_computation.4 | loop fusion | flops 1048576 | bytes 4194304 | tf_op jit(solution)/shard_map/stack | solution.py:43
  42.9 0.0 reduce-scatter.2.cloned.1.call-update
  42.9 0.0 copy-start.1
  42.9 57.5 %reduce-scatter.2.cloned.1.call-done = bf16[2,512,128]{2,1,0:T(8,128)(2,1)} async-done(((bf16[2,4096,128]{2,1,0:T(8,128)(2,1)}), bf16[2,512,128]{2,1,0:T(8,128)(2,1)}) %reduce-scatter.2.cloned.1.call-update) | async-done | bytes 262160 | tf_op jit(solution)/shard_map/reduce_scatter | solution.py:42
  100.4 1.1 convert_element_type.56
  101.5 0.3 copy.16
  101.7 18.9 %all_to_all.10 = bf16[2,16,4096]{2,0,1:T(2,128)(2,1)S(1)} all-to-all(bf16[2,16,4096]{2,0,1:T(2,128)(2,1)S(1)} %copy.16), channel_id=1, replica_groups=mesh['section'=16,'dp'=8,'tensor'=8] {'section'}, dimensions={1} | all-to-all | bytes 524288 | tf_op jit(solution)/shard_map/all_to_all | solution.py:51
  120.6 0.9 rev.14
  121.5 3.5 %all-to-all-start.1 = ((bf16[2,16,4096]{2,0,1:T(2,128)(2,1)}), bf16[2,16,4096]{2,0,1:T(2,128)(2,1)S(1)}, u32[]{:S(2)}, u32[]{:S(2)}) async-start(bf16[2,16,4096]{2,0,1:T(2,128)(2,1)} %rev.14), calls=%async_computation.2 | async-start | bytes 524288 | tf_op jit(solution)/shard_map/all_to_all | solution.py:51
  125.1 0.0 copy-done
  125.1 1.0 fusion.2
  126.0 0.0 copy-done.1
  126.0 1.0 fusion.3
  127.0 0.0 copy-start.2
  127.0 8.8 %all-to-all-done.1 = bf16[2,16,4096]{2,0,1:T(2,128)(2,1)S(1)} async-done(((bf16[2,16,4096]{2,0,1:T(2,128)(2,1)}), bf16[2,16,4096]{2,0,1:T(2,128)(2,1)S(1)}, u32[]{:S(2)}, u32[]{:S(2)}) %all-to-all-start.1) | async-done | bytes 262176 | tf_op jit(solution)/shard_map/all_to_all | solution.py:51
  135.8 0.2 copy_convert_fusion
  135.9 0.1 reshape.76
  136.0 0.0 copy-done.2
  136.0 0.0 copy-done.3
  136.0 2.5 %divide_subtract_fusion = (f32[1,2,512,128]{3,2,1,0:T(8,128)}, f32[1,2,512,128]{3,2,1,0:T(8,128)}, f32[1,2,512,128]{3,2,1,0:T(8,128)}) fusion(f32[1,2,512,128]{3,2,1,0:T(8,128)S(1)} %copy-done.2, f32[2,512,128]{2,1,0:T(8,128)S(1)} %reshape.76, bf16[2,512,128]{2,1,0:T(8,128)(2,1)} %reduce-scatter.2.cloned.1.call-done, f32[1,2,512,128]{3,2,1,0:T(8,128)S(1)} %copy-done.3, ...), kind=kLoop, calls=%fused_computation.25 | loop fusion | flops 1835008 | bytes 3932160 | tf_op jit(solution)/shard_map/sub | solution.py:62
  (3 shorter events, 0.0 us)
Async XLA Ops:
  7.2 117.9 %copy-start = (bf16[1,4096,128]{2,1,0:T(8,128)(2,1)S(1)}, bf16[1,4096,128]{2,1,0:T(8,128)(2,1)}, u32[]{:S(2)}) copy-start(bf16[1,4096,128]{2,1,0:T(8,128)(2,1)} %param.13) | copy-start | bytes 3145732
  7.2 33.6 %copy-start.4 = (bf16[1,64,128]{2,1,0:T(8,128)(2,1)S(1)}, bf16[1,64,128]{2,1,0:T(8,128)(2,1)}, u32[]{:S(2)}) copy-start(bf16[1,64,128]{2,1,0:T(8,128)(2,1)} %param.12) | copy-start | bytes 49156
  7.2 93.2 %reduce-scatter.2.cloned.1.call-start = ((), (), s32[]{:S(2)}) async-start(), calls=%async_computation.3 | async-start | bytes 2359296 | tf_op jit(solution)/shard_map/reduce_scatter | solution.py:42
  7.2 28.0 %collective-permute-start = (bf16[1,64,4096]{2,1,0:T(8,128)(2,1)}, bf16[1,64,4096]{2,1,0:T(8,128)(2,1)S(1)}, u32[]{:S(2)}, u32[]{:S(2)}) collective-permute-start(bf16[1,64,4096]{2,1,0:T(8,128)(2,1)} %param.9), channel_id=1, source_target_pairs={{960,0},{0,64},{64,128},{128,192},{192,256},{256,320},{320,384},{3... | collective-permute-start | bytes 1572872 | tf_op jit(solution)/shard_map/ppermute | solution.py:12
  12.6 26.7 %collective-permute-start.1 = (bf16[1,64,4096]{2,1,0:T(8,128)(2,1)}, bf16[1,64,4096]{2,1,0:T(8,128)(2,1)S(1)}, u32[]{:S(2)}, u32[]{:S(2)}) collective-permute-start(bf16[1,64,4096]{2,1,0:T(8,128)(2,1)} %param.10), channel_id=1, source_target_pairs={{64,0},{128,64},{192,128},{256,192},{320,256},{384,320},{448,384},... | collective-permute-start | bytes 1572872 | tf_op jit(solution)/shard_map/ppermute | solution.py:12
  42.9 83.1 %copy-start.1 = (bf16[1,4096,128]{2,1,0:T(8,128)(2,1)S(1)}, bf16[1,4096,128]{2,1,0:T(8,128)(2,1)}, u32[]{:S(2)}) copy-start(bf16[1,4096,128]{2,1,0:T(8,128)(2,1)} %param.14) | copy-start | bytes 3145732
  121.5 14.3 %all-to-all-start.1 = ((bf16[2,16,4096]{2,0,1:T(2,128)(2,1)}), bf16[2,16,4096]{2,0,1:T(2,128)(2,1)S(1)}, u32[]{:S(2)}, u32[]{:S(2)}) async-start(bf16[2,16,4096]{2,0,1:T(2,128)(2,1)} %rev.14), calls=%async_computation.2 | async-start | bytes 524288 | tf_op jit(solution)/shard_map/all_to_all | solution.py:51
  127.0 9.0 %copy-start.2 = (f32[1,2,512,128]{3,2,1,0:T(8,128)S(1)}, f32[1,2,512,128]{3,2,1,0:T(8,128)}, u32[]{:S(2)}) copy-start(f32[1,2,512,128]{3,2,1,0:T(8,128)} %param.15) | copy-start | bytes 1572868
  127.0 9.1 %copy-start.3 = (f32[1,2,512,128]{3,2,1,0:T(8,128)S(1)}, f32[1,2,512,128]{3,2,1,0:T(8,128)}, u32[]{:S(2)}) copy-start(f32[1,2,512,128]{3,2,1,0:T(8,128)} %param.16) | copy-start | bytes 1572868
Sparse Core Ops, SparseCore 0:
  43.0 57.3 reduce-scatter.1
where the time goes:
time: 146 us; the launch traced here: 145 us
  waiting for transfers between devices  87.2 us (60%)
  blocking collectives  18.9 us (13%)
  starting transfers between devices  14.5 us (10%)
  between operations  14.1 us (10%)
  other arithmetic  4.58 us (3%)
  matrix products  3.74 us (3%)
  local copies, waits for them, and re-layouts  2.35 us (2%)
    reduce_scatter x1, waiting for transfers between devices, shards(): lax.psum_scatter(jnp.stack([partial_down, partial_up]).astype(jnp.bfloat1...  57.5 us
    ppermute x2, waiting for transfers between devices, passed_along(): return lax.ppermute(block, axis, route)  20.9 us
    all_to_all x1, blocking collectives, shards(): lax.all_to_all(pieces.astype(jnp.bfloat16), 'section', split_axis=1, conc...  18.9 us
    ppermute x2, starting transfers between devices, passed_along(): return lax.ppermute(block, axis, route)  10.9 us
    all_to_all x1, waiting for transfers between devices, shards(): lax.all_to_all(pieces.astype(jnp.bfloat16), 'section', split_axis=1, conc...  8.79 us
    all_to_all x1, starting transfers between devices, shards(): lax.all_to_all(pieces.astype(jnp.bfloat16), 'section', split_axis=1, conc...  3.53 us
  transfers between devices with their start and end apart: 4, of which 4 were waited for; matrix products, arithmetic and copies ran while one was open for 1% of the time, Pallas kernels for 0%

commit v1 on v0

v1 whole, which is shorter than its diff:
```python
import functools
import jax
import jax.numpy as jnp
from jax import lax
from jax.experimental import pallas as pl
from jax.experimental.pallas import tpu as pltpu
from jax.sharding import PartitionSpec as P

STEP = 20
MESH = pl.DeviceIdType.MESH


def relay_kernel(
    down_hidden, up_hidden, down_cot, up_cot, down_weight, up_weight,
    totals, down_values, up_values,
    raw, normed, feats, cots, weights, grad_out, grad_in, part_out, part_in,
    load_sem, relay_send, relay_recv, cot_send, cot_recv, ring_send, right_recv, left_recv,
    part_send, part_recv, grad_send, grad_recv,
):
    sections, dp, tensor = (lax.axis_size(a) for a in ("section", "dp", "tensor"))
    s, d, t = (lax.axis_index(a) for a in ("section", "dp", "tensor"))
    rows = raw.shape[1]
    blocks = feats.shape[2]
    onward = (lax.rem(s + 1, sections), lax.rem(s + sections - 1, sections))
    right, left = lax.rem(t + 1, tensor), lax.rem(t + tensor - 1, tensor)
    mirror = sections - 1 - s
    group, half = lax.div(t, 2), lax.rem(t, 2)

    loads = []
    for way, source in enumerate((down_hidden, up_hidden)):
        loads.append(pltpu.make_async_copy(source.at[group], raw.at[way], load_sem.at[way]))
    for way, source in enumerate((down_cot, up_cot)):
        loads.append(pltpu.make_async_copy(source, cots.at[d, way], load_sem.at[2 + way]))
    for way, source in enumerate((down_weight, up_weight)):
        loads.append(pltpu.make_async_copy(source.at[d], weights.at[way], load_sem.at[4 + way]))
    for load in loads:
        load.start()

    barrier = pltpu.get_barrier_semaphore()
    for peer in range(dp):
        for way in range(2):
            pl.semaphore_signal(barrier, device_id={"section": onward[way], "dp": peer}, device_id_type=MESH)
    for step in range(1, dp):
        pl.semaphore_signal(barrier, device_id={"dp": lax.rem(d + step, dp)}, device_id_type=MESH)
    pl.semaphore_signal(barrier, device_id={"tensor": right}, device_id_type=MESH)
    pl.semaphore_signal(barrier, device_id={"tensor": left}, device_id_type=MESH)
    pl.semaphore_signal(barrier, device_id={"section": mirror}, device_id_type=MESH)

    for way in range(2):
        loads[way].wait()
        values = raw[way].astype(jnp.float32)
        factor = lax.rsqrt(jnp.mean(values * values, axis=-1, keepdims=True) + 1e-05)
        scaled = (values * factor).astype(jnp.bfloat16)
        for block in range(normed.shape[1]):
            normed[way, block] = scaled[:, block * 128 : (block + 1) * 128]
    pl.semaphore_wait(barrier, 2 * dp + dp - 1 + 3)

    for way in range(2):
        for peer in range(dp):
            pltpu.make_async_remote_copy(
                src_ref=normed.at[way, pl.ds((peer * 2 + half) * blocks, blocks)],
                dst_ref=feats.at[way, t, :, d],
                send_sem=relay_send,
                recv_sem=relay_recv.at[way],
                device_id={"section": onward[way], "dp": peer},
                device_id_type=MESH,
            ).start()
    loads[2].wait()
    loads[3].wait()
    for step in range(1, dp):
        pltpu.make_async_remote_copy(
            src_ref=cots.at[d],
            dst_ref=cots.at[d],
            send_sem=cot_send,
            recv_sem=cot_recv,
            device_id={"dp": lax.rem(d + step, dp)},
            device_id_type=MESH,
        ).start()
    loads[4].wait()
    loads[5].wait()

    half_ring = tensor // 2
    hops = ((half_ring, tensor - 1 - half_ring), (tensor - 1 - half_ring, half_ring))

    def send_on(way, block, step, rightward):
        origin = lax.rem(t + tensor - step, tensor) if rightward else lax.rem(t + step, tensor)
        recv = right_recv if rightward else left_recv
        piece = feats.at[way, origin, block]
        return pltpu.make_async_remote_copy(
            src_ref=piece,
            dst_ref=piece,
            send_sem=ring_send,
            recv_sem=recv.at[way, block, step],
            device_id={"tensor": right if rightward else left},
            device_id_type=MESH,
        )

    def arrived(way, block, step, rightward):
        origin = lax.rem(t + 2 * tensor - step - 1, tensor) if rightward else lax.rem(t + step + 1, tensor)
        recv = right_recv if rightward else left_recv
        piece = feats.at[way, origin, block]
        pltpu.make_async_copy(piece, piece, recv.at[way, block, step]).wait()

    def gradient(way, block):
        features = jnp.concatenate(
            [
                jnp.concatenate([feats[way, 2 * g + h, block].reshape(-1, 128) for g in range(tensor // 2)], axis=0)
                for h in range(2)
            ],
            axis=1,
        )
        cot = jnp.concatenate([cots[:, way, g].reshape(-1, 128) for g in range(tensor // 2)], axis=0)
        grad = lax.dot_general(features, cot, (((0,), (0,)), ((), ())), preferred_element_type=jnp.float32)
        grad = grad.reshape(2, 128, 128)
        totals[way, :, block] = grad
        grad_out[way, block] = grad.astype(jnp.bfloat16)
        mirrored(way, block).start()

    def mirrored(way, block):
        return pltpu.make_async_remote_copy(
            src_ref=grad_out.at[way, block],
            dst_ref=grad_in.at[way, block],
            send_sem=grad_send.at[way, block],
            recv_sem=grad_recv.at[way, block],
            device_id={"section": mirror},
            device_id_type=MESH,
        )

    def project(way):
        for g in range(tensor // 2):
            features = jnp.concatenate(
                [feats[way, 2 * g + h, block].reshape(-1, 128) for h in range(2) for block in range(blocks)], axis=1
            )
            part = jnp.dot(features, weights[way], preferred_element_type=jnp.float32)
            part_out[way, :, g] = part.astype(jnp.bfloat16).reshape(dp, rows, 128)
        for step in range(1, dp):
            peer = lax.rem(d + step, dp)
            pltpu.make_async_remote_copy(
                src_ref=part_out.at[way, peer],
                dst_ref=part_in.at[way, step - 1],
                send_sem=part_send,
                recv_sem=part_recv.at[way],
                device_id={"dp": peer},
                device_id_type=MESH,
            ).start()

    stages = [(way, block) for way in range(2) for block in range(blocks)]
    events = []
    for index, (way, block) in enumerate(stages):
        for step in range(half_ring + 1):
            events.append((index + step, step, index))
    for _, step, index in sorted(events, key=lambda e: (e[0], -e[1])):
        way, block = stages[index]
        if step == 0:
            if block == 0:
                pltpu.make_async_copy(feats.at[way, t], feats.at[way, t], relay_recv.at[way]).wait()
        for rightward in (True, False):
            limit = hops[way][0 if rightward else 1]
            if 1 <= step <= limit:
                arrived(way, block, step - 1, rightward)
            if step < limit:
                send_on(way, block, step, rightward).start()
        if step == half_ring:
            if index == 0:
                pltpu.make_async_copy(cots.at[pl.ds(0, dp - 1)], cots.at[pl.ds(0, dp - 1)], cot_recv).wait()
            gradient(way, block)
            if block == blocks - 1:
                project(way)

    for way in range(2):
        for block in range(blocks):
            mirrored(way, block).wait_recv()
            totals[1 - way, :, block] += grad_in[way, block].astype(jnp.float32)
        pltpu.make_async_copy(part_in.at[way], part_in.at[way], part_recv.at[way]).wait()
        total = part_out[way, d].astype(jnp.float32)
        for step in range(dp - 1):
            total += part_in[way, step].astype(jnp.float32)
        (down_values, up_values)[way][...] = total.astype(jnp.bfloat16)

    sent = normed.at[:, pl.ds(0, dp * blocks)]
    pltpu.make_async_copy(sent, sent, relay_send).wait()
    pltpu.make_async_copy(cots.at[pl.ds(0, dp - 1)], cots.at[pl.ds(0, dp - 1)], cot_send).wait()
    sent = feats.at[:, pl.ds(0, tensor - 1)]
    pltpu.make_async_copy(sent, sent, ring_send).wait()
    pltpu.make_async_copy(part_in, part_in, part_send).wait()
    for way in range(2):
        for block in range(blocks):
            mirrored(way, block).wait_send()


def shards(
    down_hidden, up_hidden, down_cot, up_cot, down_weight, up_weight, master, moment1, moment2
):
    sections, dp, tensor = (lax.axis_size(a) for a in ("section", "dp", "tensor"))
    tokens, width = down_hidden.shape[1:]
    groups = tensor // 2
    rows = tokens // groups
    shard = width // dp
    blocks = shard // 2 // 128
    hbm = pl.BlockSpec(memory_space=pltpu.HBM)
    vmem = pl.BlockSpec(memory_space=pltpu.VMEM)
    bf16, f32 = jnp.bfloat16, jnp.float32
    DMA = pltpu.SemaphoreType.DMA
    totals, down_values, up_values = pl.pallas_call(
        relay_kernel,
        out_shape=(
            jax.ShapeDtypeStruct((2, 2, blocks, 128, 128), f32),
            jax.ShapeDtypeStruct((groups, rows, 128), bf16),
            jax.ShapeDtypeStruct((groups, rows, 128), bf16),
        ),
        in_specs=[hbm] * 6,
        out_specs=(vmem, vmem, vmem),
        scratch_shapes=[
            pltpu.VMEM((2, rows, width), bf16),
            pltpu.VMEM((2, width // 128, rows, 128), bf16),
            pltpu.VMEM((2, tensor, blocks, dp, rows, 128), bf16),
            pltpu.VMEM((dp, 2, groups, rows, 128), bf16),
            pltpu.VMEM((2, shard, 128), bf16),
            pltpu.VMEM((2, blocks, 2, 128, 128), bf16),
            pltpu.VMEM((2, blocks, 2, 128, 128), bf16),
            pltpu.VMEM((2, dp, groups, rows, 128), bf16),
            pltpu.VMEM((2, dp - 1, groups, rows, 128), bf16),
            DMA((6,)),
            DMA,
            DMA((2,)),
            DMA,
            DMA,
            DMA,
            DMA((2, blocks, tensor // 2)),
            DMA((2, blocks, tensor // 2)),
            DMA,
            DMA((2,)),
            DMA((2, blocks)),
            DMA((2, blocks)),
        ],
        compiler_params=pltpu.CompilerParams(
            collective_id=0, has_side_effects=True, vmem_limit_bytes=60 * 1024 * 1024
        ),
    )(
        down_hidden.reshape(groups, rows, width),
        up_hidden.reshape(groups, rows, width),
        down_cot.reshape(groups, rows, 128),
        up_cot.reshape(groups, rows, 128),
        down_weight.reshape(dp, shard, 128),
        up_weight.reshape(dp, shard, 128),
    )
    totals = totals.reshape(master.shape)
    new_moment1 = 0.9 * moment1 + 0.1 * totals
    new_moment2 = 0.95 * moment2 + 0.05 * totals * totals
    first_fix = 1.0 - 0.9**STEP
    second_fix = 1.0 - 0.95**STEP
    new_master = master - 0.05 * (new_moment1 / first_fix) / (
        jnp.sqrt(new_moment2 / second_fix) + 1e-08
    )
    return (
        down_values.reshape(down_cot.shape),
        up_values.reshape(up_cot.shape),
        new_master,
        new_moment1,
        new_moment2,
    )


def solution(mesh):
    return jax.shard_map(
        shards,
        mesh=mesh,
        in_specs=(
            P("section", "dp", None),
            P("section", "dp", None),
            P("section", "dp", "tensor"),
            P("section", "dp", "tensor"),
            P("section", None, "tensor"),
            P("section", None, "tensor"),
            P("section", None, "dp", "tensor"),
            P("section", None, "dp", "tensor"),
            P("section", None, "dp", "tensor"),
        ),
        out_specs=(
            P("section", "dp", "tensor"),
            P("section", "dp", "tensor"),
            P("section", None, "dp", "tensor"),
            P("section", None, "dp", "tensor"),
            P("section", None, "dp", "tensor"),
        ),
        check_vma=False,
    )
```

time: 146 us -> 64.8 us (0.44)
  the two profiles are of different devices: /device:TPU:2 before, /device:TPU:1 now
where the time goes in v1:
time: 64.8 us; the launch traced here: 64.6 us
  Pallas kernels  60.2 us (93%)
  other arithmetic  2.37 us (4%)
  local copies, waits for them, and re-layouts  1.35 us (2%)
  between operations  0.7 us (1%)
    pallas_call x1, Pallas kernels, shards(): pl.pallas_call(relay_kernel, out_shape=(jax.ShapeDtypeStruct((2, 2, block...  60.2 us
    sub x1, other arithmetic, shards(): master - 0.05 * (new_moment1 / first_fix) / (jnp.sqrt(new_moment2 / secon...  2.37 us
    unnamed x12, local copies, waits for them, and re-layouts  1.35 us

profile of v1, /device:TPU:1, one launch (start us, length us, event | category | flops | bytes accessed | tf_op | source)
XLA Modules:
  0.0 64.6 jit_solution(1592209495006705240)
XLA Ops:
  0.6 0.0 copy-start
  0.6 0.0 copy-start.1
  0.7 0.0 copy-start.2
  0.7 60.2 %shard_map.128 = (f32[2,2,2,128,128]{4,3,2,1,0:T(8,128)}, bf16[4,16,128]{2,1,0:T(8,128)(2,1)}, bf16[4,16,128]{2,1,0:T(8,128)(2,1)}) custom-call(bf16[4,16,4096]{2,1,0:T(8,128)(2,1)} %bitcast.11, bf16[4,16,4096]{2,1,0:T(8,128)(2,1)} %bitcast.12, bf16[4,16,128]{2,1,0:T(8,128)(2,1)} %bitcast.14, bf16[4,16,128]{2,1,0:T(8,128)(2,1)} %bitcast.15, ...), custom_call_target="tpu_custom_call" | custom-call | tf_op jit(solution)/shard_map/pallas_call | solution.py:204
  60.8 0.0 copy-done
  60.9 0.0 copy-done.1
  60.9 0.0 copy-done.2
  60.9 0.0 copy-start.4
  60.9 2.4 %divide_subtract_fusion = (f32[1,2,512,128]{3,2,1,0:T(8,128)}, f32[1,2,512,128]{3,2,1,0:T(8,128)}, f32[1,2,512,128]{3,2,1,0:T(8,128)}) fusion(f32[1,2,512,128]{3,2,1,0:T(8,128)S(1)} %copy-done, f32[1,2,512,128]{3,2,1,0:T(8,128)} %bitcast.13, f32[1,2,512,128]{3,2,1,0:T(8,128)S(1)} %copy-done.1, f32[1,2,512,128]{3,2,1,0:T(8,128)S(1)} %copy-done.2), kind=kLoop, calls=%fused_computation.2 | loop fusion | flops 1572864 | bytes 3670016 | tf_op jit(solution)/shard_map/sub | solution.py:252
  63.3 0.0 copy-done.4
  63.3 0.0 copy-start.3
  63.3 0.6 copy.16
  63.9 0.1 copy-done.3
  64.0 0.6 copy.17
Async XLA Ops:
  0.6 60.2 %copy-start = (f32[1,2,512,128]{3,2,1,0:T(8,128)S(1)}, f32[1,2,512,128]{3,2,1,0:T(8,128)}, u32[]{:S(2)}) copy-start(f32[1,2,512,128]{3,2,1,0:T(8,128)} %param.15) | copy-start | bytes 1572868
  0.6 60.2 %copy-start.1 = (f32[1,2,512,128]{3,2,1,0:T(8,128)S(1)}, f32[1,2,512,128]{3,2,1,0:T(8,128)}, u32[]{:S(2)}) copy-start(f32[1,2,512,128]{3,2,1,0:T(8,128)} %param.16) | copy-start | bytes 1572868
  0.7 60.2 %copy-start.2 = (f32[1,2,512,128]{3,2,1,0:T(8,128)S(1)}, f32[1,2,512,128]{3,2,1,0:T(8,128)}, u32[]{:S(2)}) copy-start(f32[1,2,512,128]{3,2,1,0:T(8,128)} %param.17) | copy-start | bytes 1572868
  60.9 2.4 %copy-start.4 = (bf16[4,16,128]{2,1,0:T(8,128)(2,1)S(1)}, bf16[4,16,128]{2,1,0:T(8,128)(2,1)}, u32[]{:S(2)}) copy-start(bf16[4,16,128]{2,1,0:T(8,128)(2,1)} %get-tuple-element.8) | copy-start | bytes 49156
  63.3 0.7 %copy-start.3 = (bf16[4,16,128]{2,1,0:T(8,128)(2,1)S(1)}, bf16[4,16,128]{2,1,0:T(8,128)(2,1)}, u32[]{:S(2)}) copy-start(bf16[4,16,128]{2,1,0:T(8,128)(2,1)} %get-tuple-element.9) | copy-start | bytes 49156

commit v2 on v1

v2 whole, which is shorter than its diff:
```python
import functools
import jax
import jax.numpy as jnp
from jax import lax
from jax.experimental import pallas as pl
from jax.experimental.pallas import tpu as pltpu
from jax.sharding import PartitionSpec as P

STEP = 20
MESH = pl.DeviceIdType.MESH


def relay_kernel(
    down_hidden, up_hidden, down_cot, up_cot, down_weight, up_weight,
    totals, down_values, up_values,
    raw, normed, feats, cots, weights, grad_out, grad_in, part_out, part_in,
    load_sem, relay_send, relay_recv, cot_send, cot_recv, pass_recv, side_send, right_recv, left_recv,
    part_send, part_recv, grad_send, grad_recv,
):
    sections, dp, tensor = (lax.axis_size(a) for a in ("section", "dp", "tensor"))
    s, d, t = (lax.axis_index(a) for a in ("section", "dp", "tensor"))
    rows = raw.shape[2]
    groups = 4
    blocks = feats.shape[4]
    onward = (lax.rem(s + 1, sections), lax.rem(s + sections - 1, sections))
    right, left = lax.rem(t + 1, tensor), lax.rem(t + tensor - 1, tensor)
    mirror = sections - 1 - s
    sibling = d + 1 - 2 * lax.rem(d, 2)

    def kind_of(offset):
        kind = lax.rem(t + offset + 4, 4)
        return lax.rem(kind, 2), lax.div(kind, 2)

    half, pair = kind_of(0)
    other = 1 - half

    barrier = pltpu.get_barrier_semaphore()
    for way in range(2):
        for peer in range(dp):
            pl.semaphore_signal(barrier, device_id={"section": onward[way], "dp": peer}, device_id_type=MESH)
    for step in range(1, dp):
        pl.semaphore_signal(barrier, device_id={"dp": lax.rem(d + step, dp)}, device_id_type=MESH)
    pl.semaphore_signal(barrier, device_id={"tensor": right}, device_id_type=MESH)
    pl.semaphore_signal(barrier, device_id={"tensor": left}, device_id_type=MESH)
    pl.semaphore_signal(barrier, device_id={"section": mirror}, device_id_type=MESH)

    loads = []
    for way, source in enumerate((down_hidden, up_hidden)):
        for j in range(2):
            loads.append(pltpu.make_async_copy(source.at[2 * j + pair], raw.at[way, j], load_sem.at[2 * way + j]))
    for way, source in enumerate((down_cot, up_cot)):
        loads.append(pltpu.make_async_copy(source, cots.at[way, :, d], load_sem.at[4 + way]))
    for way, source in enumerate((down_weight, up_weight)):
        loads.append(pltpu.make_async_copy(source.at[d], weights.at[way], load_sem.at[6 + way]))
    for load in loads:
        load.start()

    def normalize(way):
        loads[2 * way].wait()
        loads[2 * way + 1].wait()
        for j in range(2):
            values = raw[way, j].astype(jnp.float32)
            factor = lax.rsqrt(jnp.mean(values * values, axis=-1, keepdims=True) + 1e-05)
            for peer in range(dp):
                for block in range(blocks):
                    at = pl.multiple_of(((peer * 2 + half) * blocks + block) * 128, 128)
                    chosen = raw[way, j, :, pl.ds(at, 128)].astype(jnp.float32)
                    normed[way, peer, j, block] = (chosen * factor).astype(jnp.bfloat16)

    def relay(way):
        for peer in range(dp):
            pltpu.make_async_remote_copy(
                src_ref=normed.at[way, peer],
                dst_ref=feats.at[way, half, pair, :, :, d],
                send_sem=relay_send,
                recv_sem=relay_recv.at[way],
                device_id={"section": onward[way], "dp": peer},
                device_id_type=MESH,
            ).start()

    def share_cots():
        loads[4].wait()
        loads[5].wait()
        piece = cots.at[:, :, d]
        for step in range(2, dp, 2):
            pltpu.make_async_remote_copy(
                src_ref=piece,
                dst_ref=piece,
                send_sem=cot_send,
                recv_sem=cot_recv,
                device_id={"dp": lax.rem(d + step, dp)},
                device_id_type=MESH,
            ).start()
        pass_cots(d)

    def pass_cots(owner):
        piece = cots.at[:, :, owner]
        pltpu.make_async_remote_copy(
            src_ref=piece,
            dst_ref=piece,
            send_sem=cot_send,
            recv_sem=pass_recv,
            device_id={"dp": sibling},
            device_id_type=MESH,
        ).start()

    def side(way, step, rightward):
        j = (0 if rightward else 1) if step != 1 else (1 if rightward else 0)
        h, p = kind_of(0 if step < 2 else (-1 if rightward else 1))
        piece = feats.at[way, h, p, j]
        return pltpu.make_async_remote_copy(
            src_ref=piece,
            dst_ref=piece,
            send_sem=side_send.at[way],
            recv_sem=(right_recv if rightward else left_recv).at[way, step],
            device_id={"tensor": right if rightward else left},
            device_id_type=MESH,
        )

    def side_wait(way, step):
        for rightward in (True, False):
            piece = feats.at[way, 0, 0, 0]
            pltpu.make_async_copy(piece, piece, (right_recv if rightward else left_recv).at[way, step]).wait()

    def mirrored(way, which):
        return pltpu.make_async_remote_copy(
            src_ref=grad_out.at[way, which],
            dst_ref=grad_in.at[way, which],
            send_sem=grad_send.at[way, which],
            recv_sem=grad_recv.at[way, which],
            device_id={"section": mirror},
            device_id_type=MESH,
        )

    order = [(p, j) for p in range(2) for j in range(2)]

    def gradient(way, which, position):
        features = jnp.concatenate(
            [
                jnp.concatenate([feats[way, position, p, j, block].reshape(-1, 128) for p, j in order], axis=0)
                for block in range(blocks)
            ],
            axis=1,
        )
        cot = jnp.concatenate([cots[way, 2 * j + p].reshape(-1, 128) for p, j in order], axis=0)
        grad = lax.dot_general(features, cot, (((0,), (0,)), ((), ())), preferred_element_type=jnp.float32)
        totals[way, position] = grad
        grad_out[way, which] = grad.astype(jnp.bfloat16)
        mirrored(way, which).start()

    def project(way, which):
        p = pair if which == 0 else 1 - pair
        for j in range(2):
            features = jnp.concatenate(
                [feats[way, h, p, j, block].reshape(-1, 128) for h in range(2) for block in range(blocks)], axis=1
            )
            part = jnp.dot(features, weights[way], preferred_element_type=jnp.float32)
            part_out[way, which, :, j] = part.astype(jnp.bfloat16).reshape(dp, rows, 128)
        for step in range(1, dp):
            peer = lax.rem(d + step, dp)
            pltpu.make_async_remote_copy(
                src_ref=part_out.at[way, which, peer],
                dst_ref=part_in.at[way, which, step - 1],
                send_sem=part_send,
                recv_sem=part_recv.at[way, which],
                device_id={"dp": peer},
                device_id_type=MESH,
            ).start()

    normalize(0)
    pl.semaphore_wait(barrier, 2 * dp + dp - 1 + 3)
    relay(0)
    normalize(1)
    relay(1)
    share_cots()
    loads[6].wait()
    loads[7].wait()
    for way in range(2):
        landed = feats.at[way, 0, 0]
        pltpu.make_async_copy(landed, landed, relay_recv.at[way]).wait()
        for step in range(2):
            for rightward in (True, False):
                side(way, step, rightward).start()
    got = cots.at[:, :, pl.ds(0, dp // 2 - 1)]
    pltpu.make_async_copy(got, got, cot_recv).wait()
    for step in range(2, dp, 2):
        pass_cots(lax.rem(d + step, dp))
    for way in range(2):
        side_wait(way, 0)
        for rightward in (True, False):
            side(way, 2, rightward).start()
        side_wait(way, 1)
        if way == 0:
            got = cots.at[:, :, pl.ds(0, dp // 2)]
            pltpu.make_async_copy(got, got, pass_recv).wait()
        gradient(way, 0, other)
    for way in range(2):
        project(way, 0)
    for way in range(2):
        side_wait(way, 2)
        gradient(way, 1, half)
    for way in range(2):
        project(way, 1)

    for which, position in ((0, other), (1, half)):
        for way in range(2):
            mirrored(way, which).wait_recv()
            totals[1 - way, position] += grad_in[way, which].astype(jnp.float32)
    for way in range(2):
        for which in range(2):
            got = part_in.at[way, which]
            pltpu.make_async_copy(got, got, part_recv.at[way, which]).wait()
            total = part_out[way, which, d].astype(jnp.float32)
            for step in range(dp - 1):
                total += part_in[way, which, step].astype(jnp.float32)
            total = total.astype(jnp.bfloat16)
            for j in range(2):
                (down_values, up_values)[way][2 * j + (pair if which == 0 else 1 - pair)] = total[j]

    pltpu.make_async_copy(normed, normed, relay_send).wait()
    sent = cots.at[:, :, pl.ds(0, dp - 1)]
    pltpu.make_async_copy(sent, sent, cot_send).wait()
    for way in range(2):
        sent = feats.at[way, :, :, :, :, pl.ds(0, dp * 3 // 4)]
        pltpu.make_async_copy(sent, sent, side_send.at[way]).wait()
    pltpu.make_async_copy(part_in, part_in, part_send).wait()
    for way in range(2):
        for which in range(2):
            mirrored(way, which).wait_send()


def shards(
    down_hidden, up_hidden, down_cot, up_cot, down_weight, up_weight, master, moment1, moment2
):
    sections, dp, tensor = (lax.axis_size(a) for a in ("section", "dp", "tensor"))
    tokens, width = down_hidden.shape[1:]
    groups = 4
    rows = tokens // groups
    shard = width // dp
    blocks = shard // 2 // 128
    hbm = pl.BlockSpec(memory_space=pltpu.HBM)
    vmem = pl.BlockSpec(memory_space=pltpu.VMEM)
    bf16, f32 = jnp.bfloat16, jnp.float32
    DMA = pltpu.SemaphoreType.DMA
    totals, down_values, up_values = pl.pallas_call(
        relay_kernel,
        out_shape=(
            jax.ShapeDtypeStruct((2, 2, blocks * 128, 128), f32),
            jax.ShapeDtypeStruct((groups, rows, 128), bf16),
            jax.ShapeDtypeStruct((groups, rows, 128), bf16),
        ),
        in_specs=[hbm] * 6,
        out_specs=(vmem, vmem, vmem),
        scratch_shapes=[
            pltpu.VMEM((2, 2, rows, width), bf16),
            pltpu.VMEM((2, dp, 2, blocks, rows, 128), bf16),
            pltpu.VMEM((2, 2, 2, 2, blocks, dp, rows, 128), bf16),
            pltpu.VMEM((2, groups, dp, rows, 128), bf16),
            pltpu.VMEM((2, shard, 128), bf16),
            pltpu.VMEM((2, 2, blocks * 128, 128), bf16),
            pltpu.VMEM((2, 2, blocks * 128, 128), bf16),
            pltpu.VMEM((2, 2, dp, 2, rows, 128), bf16),
            pltpu.VMEM((2, 2, dp - 1, 2, rows, 128), bf16),
            DMA((8,)),
            DMA,
            DMA((2,)),
            DMA,
            DMA,
            DMA,
            DMA((2,)),
            DMA((2, 3)),
            DMA((2, 3)),
            DMA,
            DMA((2, 2)),
            DMA((2, 2)),
            DMA((2, 2)),
        ],
        compiler_params=pltpu.CompilerParams(
            collective_id=0, has_side_effects=True, vmem_limit_bytes=60 * 1024 * 1024
        ),
    )(
        down_hidden.reshape(groups, rows, width),
        up_hidden.reshape(groups, rows, width),
        down_cot.reshape(groups, rows, 128),
        up_cot.reshape(groups, rows, 128),
        down_weight.reshape(dp, shard, 128),
        up_weight.reshape(dp, shard, 128),
    )
    totals = totals.reshape(master.shape)
    new_moment1 = 0.9 * moment1 + 0.1 * totals
    new_moment2 = 0.95 * moment2 + 0.05 * totals * totals
    first_fix = 1.0 - 0.9**STEP
    second_fix = 1.0 - 0.95**STEP
    new_master = master - 0.05 * (new_moment1 / first_fix) / (
        jnp.sqrt(new_moment2 / second_fix) + 1e-08
    )
    return (
        down_values.reshape(down_cot.shape),
        up_values.reshape(up_cot.shape),
        new_master,
        new_moment1,
        new_moment2,
    )


def solution(mesh):
    return jax.shard_map(
        shards,
        mesh=mesh,
        in_specs=(
            P("section", "dp", None),
            P("section", "dp", None),
            P("section", "dp", "tensor"),
            P("section", "dp", "tensor"),
            P("section", None, "tensor"),
            P("section", None, "tensor"),
            P("section", None, "dp", "tensor"),
            P("section", None, "dp", "tensor"),
            P("section", None, "dp", "tensor"),
        ),
        out_specs=(
            P("section", "dp", "tensor"),
            P("section", "dp", "tensor"),
            P("section", None, "dp", "tensor"),
            P("section", None, "dp", "tensor"),
            P("section", None, "dp", "tensor"),
        ),
        check_vma=False,
    )
```

time: 64.8 us -> 57.4 us (0.89)
  Pallas kernels: 60.2 us -> 52.8 us
    pallas_call x1, Pallas kernels: 60.2 us -> 52.8 us  [shards(): pl.pallas_call(relay_kernel, out_shape=(jax.ShapeDtypeStruct((2, 2, block...]
where the time goes in v2:
time: 57.4 us; the launch traced here: 57.2 us
  Pallas kernels  52.8 us (92%)
  other arithmetic  2.37 us (4%)
  local copies, waits for them, and re-layouts  1.35 us (2%)
  between operations  0.7 us (1%)
    pallas_call x1, Pallas kernels, shards(): pl.pallas_call(relay_kernel, out_shape=(jax.ShapeDtypeStruct((2, 2, block...  52.8 us
    sub x1, other arithmetic, shards(): master - 0.05 * (new_moment1 / first_fix) / (jnp.sqrt(new_moment2 / secon...  2.37 us
    unnamed x12, local copies, waits for them, and re-layouts  1.35 us

profile of v2, /device:TPU:1, one launch (start us, length us, event | category | flops | bytes accessed | tf_op | source)
XLA Modules:
  0.0 57.2 jit_solution(1813133839897446036)
XLA Ops:
  0.6 0.0 copy-start
  0.6 0.0 copy-start.1
  0.7 0.0 copy-start.2
  0.7 52.8 %shard_map.128 = (f32[2,2,256,128]{3,2,1,0:T(8,128)}, bf16[4,16,128]{2,1,0:T(8,128)(2,1)}, bf16[4,16,128]{2,1,0:T(8,128)(2,1)}) custom-call(bf16[4,16,4096]{2,1,0:T(8,128)(2,1)} %bitcast.11, bf16[4,16,4096]{2,1,0:T(8,128)(2,1)} %bitcast.12, bf16[4,16,128]{2,1,0:T(8,128)(2,1)} %bitcast.14, bf16[4,16,128]{2,1,0:T(8,128)(2,1)} %bitcast.15, ...), custom_call_target="tpu_custom_call" | custom-call | tf_op jit(solution)/shard_map/pallas_call | solution.py:245
  53.5 0.0 copy-done
  53.5 0.0 copy-done.1
  53.5 0.0 copy-done.2
  53.5 0.0 copy-start.4
  53.5 2.4 %divide_subtract_fusion = (f32[1,2,512,128]{3,2,1,0:T(8,128)}, f32[1,2,512,128]{3,2,1,0:T(8,128)}, f32[1,2,512,128]{3,2,1,0:T(8,128)}) fusion(f32[1,2,512,128]{3,2,1,0:T(8,128)S(1)} %copy-done, f32[1,2,512,128]{3,2,1,0:T(8,128)} %bitcast.13, f32[1,2,512,128]{3,2,1,0:T(8,128)S(1)} %copy-done.1, f32[1,2,512,128]{3,2,1,0:T(8,128)S(1)} %copy-done.2), kind=kLoop, calls=%fused_computation.2 | loop fusion | flops 1572864 | bytes 3670016 | tf_op jit(solution)/shard_map/sub | solution.py:294
  55.9 0.0 copy-done.4
  55.9 0.0 copy-start.3
  55.9 0.6 %copy.16 = bf16[1,64,128]{2,1,0:T(8,128)(2,1)} copy(bf16[1,64,128]{2,1,0:T(8,128)(2,1)S(1)} %bitcast.17) | data formatting | bytes 32768
  56.5 0.1 copy-done.3
  56.6 0.6 %copy.17 = bf16[1,64,128]{2,1,0:T(8,128)(2,1)} copy(bf16[1,64,128]{2,1,0:T(8,128)(2,1)S(1)} %bitcast.16) | data formatting | bytes 32768
Async XLA Ops:
  0.6 52.8 %copy-start = (f32[1,2,512,128]{3,2,1,0:T(8,128)S(1)}, f32[1,2,512,128]{3,2,1,0:T(8,128)}, u32[]{:S(2)}) copy-start(f32[1,2,512,128]{3,2,1,0:T(8,128)} %param.15) | copy-start | bytes 1572868
  0.6 52.8 %copy-start.1 = (f32[1,2,512,128]{3,2,1,0:T(8,128)S(1)}, f32[1,2,512,128]{3,2,1,0:T(8,128)}, u32[]{:S(2)}) copy-start(f32[1,2,512,128]{3,2,1,0:T(8,128)} %param.16) | copy-start | bytes 1572868
  0.7 52.8 %copy-start.2 = (f32[1,2,512,128]{3,2,1,0:T(8,128)S(1)}, f32[1,2,512,128]{3,2,1,0:T(8,128)}, u32[]{:S(2)}) copy-start(f32[1,2,512,128]{3,2,1,0:T(8,128)} %param.17) | copy-start | bytes 1572868
  53.5 2.4 %copy-start.4 = (bf16[4,16,128]{2,1,0:T(8,128)(2,1)S(1)}, bf16[4,16,128]{2,1,0:T(8,128)(2,1)}, u32[]{:S(2)}) copy-start(bf16[4,16,128]{2,1,0:T(8,128)(2,1)} %get-tuple-element.8) | copy-start | bytes 49156
  55.9 0.7 %copy-start.3 = (bf16[4,16,128]{2,1,0:T(8,128)(2,1)S(1)}, bf16[4,16,128]{2,1,0:T(8,128)(2,1)}, u32[]{:S(2)}) copy-start(bf16[4,16,128]{2,1,0:T(8,128)(2,1)} %get-tuple-element.9) | copy-start | bytes 49156

commit v3 on v2

--- a/solution.py
+++ b/solution.py
@@ -21,7 +21,7 @@
     s, d, t = (lax.axis_index(a) for a in ("section", "dp", "tensor"))
     rows = raw.shape[2]
     groups = 4
-    blocks = feats.shape[4]
+    blocks = feats.shape[5]
     onward = (lax.rem(s + 1, sections), lax.rem(s + sections - 1, sections))
     right, left = lax.rem(t + 1, tensor), lax.rem(t + tensor - 1, tensor)
     mirror = sections - 1 - s
@@ -49,7 +49,7 @@
         for j in range(2):
             loads.append(pltpu.make_async_copy(source.at[2 * j + pair], raw.at[way, j], load_sem.at[2 * way + j]))
     for way, source in enumerate((down_cot, up_cot)):
-        loads.append(pltpu.make_async_copy(source, cots.at[way, :, d], load_sem.at[4 + way]))
+        loads.append(pltpu.make_async_copy(source, cots.at[d, way], load_sem.at[4 + way]))
     for way, source in enumerate((down_weight, up_weight)):
         loads.append(pltpu.make_async_copy(source.at[d], weights.at[way], load_sem.at[6 + way]))
     for load in loads:
@@ -71,7 +71,7 @@
         for peer in range(dp):
             pltpu.make_async_remote_copy(
                 src_ref=normed.at[way, peer],
-                dst_ref=feats.at[way, half, pair, :, :, d],
+                dst_ref=feats.at[way, half, pair, d],
                 send_sem=relay_send,
                 recv_sem=relay_recv.at[way],
                 device_id={"section": onward[way], "dp": peer},
@@ -81,7 +81,7 @@
     def share_cots():
         loads[4].wait()
         loads[5].wait()
-        piece = cots.at[:, :, d]
+        piece = cots.at[d]
         for step in range(2, dp, 2):
             pltpu.make_async_remote_copy(
                 src_ref=piece,
@@ -94,7 +94,7 @@
         pass_cots(d)
 
     def pass_cots(owner):
-        piece = cots.at[:, :, owner]
+        piece = cots.at[owner]
         pltpu.make_async_remote_copy(
             src_ref=piece,
             dst_ref=piece,
@@ -105,9 +105,9 @@
         ).start()
 
     def side(way, step, rightward):
-        j = (0 if rightward else 1) if step != 1 else (1 if rightward else 0)
+        part = (0 if rightward else 1) if step != 1 else (1 if rightward else 0)
         h, p = kind_of(0 if step < 2 else (-1 if rightward else 1))
-        piece = feats.at[way, h, p, j]
+        piece = feats.at[way, h, p, pl.ds(part * (dp // 2), dp // 2)]
         return pltpu.make_async_remote_copy(
             src_ref=piece,
             dst_ref=piece,
@@ -119,7 +119,7 @@
 
     def side_wait(way, step):
         for rightward in (True, False):
-            piece = feats.at[way, 0, 0, 0]
+            piece = feats.at[way, 0, 0, pl.ds(0, dp // 2)]
             pltpu.make_async_copy(piece, piece, (right_recv if rightward else left_recv).at[way, step]).wait()
 
     def mirrored(way, which):
@@ -137,12 +137,12 @@
     def gradient(way, which, position):
         features = jnp.concatenate(
             [
-                jnp.concatenate([feats[way, position, p, j, block].reshape(-1, 128) for p, j in order], axis=0)
+                jnp.concatenate([feats[way, position, p, :, j, block].reshape(-1, 128) for p, j in order], axis=0)
                 for block in range(blocks)
             ],
             axis=1,
         )
-        cot = jnp.concatenate([cots[way, 2 * j + p].reshape(-1, 128) for p, j in order], axis=0)
+        cot = jnp.concatenate([cots[:, way, 2 * j + p].reshape(-1, 128) for p, j in order], axis=0)
         grad = lax.dot_general(features, cot, (((0,), (0,)), ((), ())), preferred_element_type=jnp.float32)
         totals[way, position] = grad
         grad_out[way, which] = grad.astype(jnp.bfloat16)
@@ -152,7 +152,7 @@
         p = pair if which == 0 else 1 - pair
         for j in range(2):
             features = jnp.concatenate(
-                [feats[way, h, p, j, block].reshape(-1, 128) for h in range(2) for block in range(blocks)], axis=1
+                [feats[way, h, p, :, j, block].reshape(-1, 128) for h in range(2) for block in range(blocks)], axis=1
             )
             part = jnp.dot(features, weights[way], preferred_element_type=jnp.float32)
             part_out[way, which, :, j] = part.astype(jnp.bfloat16).reshape(dp, rows, 128)
@@ -181,7 +181,7 @@
         for step in range(2):
             for rightward in (True, False):
                 side(way, step, rightward).start()
-    got = cots.at[:, :, pl.ds(0, dp // 2 - 1)]
+    got = cots.at[pl.ds(0, dp // 2 - 1)]
     pltpu.make_async_copy(got, got, cot_recv).wait()
     for step in range(2, dp, 2):
         pass_cots(lax.rem(d + step, dp))
@@ -191,7 +191,7 @@
             side(way, 2, rightward).start()
         side_wait(way, 1)
         if way == 0:
-            got = cots.at[:, :, pl.ds(0, dp // 2)]
+            got = cots.at[pl.ds(0, dp // 2)]
             pltpu.make_async_copy(got, got, pass_recv).wait()
         gradient(way, 0, other)
     for way in range(2):
@@ -218,15 +218,47 @@
                 (down_values, up_values)[way][2 * j + (pair if which == 0 else 1 - pair)] = total[j]
 
     pltpu.make_async_copy(normed, normed, relay_send).wait()
-    sent = cots.at[:, :, pl.ds(0, dp - 1)]
+    sent = cots.at[pl.ds(0, dp - 1)]
     pltpu.make_async_copy(sent, sent, cot_send).wait()
     for way in range(2):
-        sent = feats.at[way, :, :, :, :, pl.ds(0, dp * 3 // 4)]
+        sent = feats.at[way, :, :, pl.ds(0, dp * 3 // 4)]
         pltpu.make_async_copy(sent, sent, side_send.at[way]).wait()
     pltpu.make_async_copy(part_in, part_in, part_send).wait()
     for way in range(2):
         for which in range(2):
             mirrored(way, which).wait_send()
+
+
+def adam_kernel(
+    down_values, up_values, totals, master, moment1, moment2,
+    down_out, up_out, new_master, new_moment1, new_moment2, held, value_sem, held_sem,
+):
+    moves = [
+        pltpu.make_async_copy(down_values, down_out, value_sem.at[0]),
+        pltpu.make_async_copy(up_values, up_out, value_sem.at[1]),
+    ]
+    for move in moves:
+        move.start()
+    first_fix = 1.0 - 0.9**STEP
+    second_fix = 1.0 - 0.95**STEP
+    for replica in range(2):
+        for part in range(totals.shape[1]):
+            total = totals[replica, part]
+            first = 0.9 * moment1[replica, part] + 0.1 * total
+            second = 0.95 * moment2[replica, part] + 0.05 * total * total
+            held[0, replica, part] = master[replica, part] - 0.05 * (first / first_fix) / (
+                jnp.sqrt(second / second_fix) + 1e-08
+            )
+            held[1, replica, part] = first
+            held[2, replica, part] = second
+            for index, target in enumerate((new_master, new_moment1, new_moment2)):
+                move = pltpu.make_async_copy(
+                    held.at[index, replica, part], target.at[replica, part], held_sem.at[index, replica, part]
+                )
+                move.start()
+                moves.append(move)
+    for move in moves:
+        move.wait()
 
 
 def shards(
@@ -245,17 +277,17 @@
     totals, down_values, up_values = pl.pallas_call(
         relay_kernel,
         out_shape=(
-            jax.ShapeDtypeStruct((2, 2, blocks * 128, 128), f32),
-            jax.ShapeDtypeStruct((groups, rows, 128), bf16),
-            jax.ShapeDtypeStruct((groups, rows, 128), bf16),
+            pltpu.VMEM((2, 2, blocks * 128, 128), f32),
+            pltpu.VMEM((groups, rows, 128), bf16),
+            pltpu.VMEM((groups, rows, 128), bf16),
         ),
         in_specs=[hbm] * 6,
         out_specs=(vmem, vmem, vmem),
         scratch_shapes=[
             pltpu.VMEM((2, 2, rows, width), bf16),
             pltpu.VMEM((2, dp, 2, blocks, rows, 128), bf16),
-            pltpu.VMEM((2, 2, 2, 2, blocks, dp, rows, 128), bf16),
-            pltpu.VMEM((2, groups, dp, rows, 128), bf16),
+            pltpu.VMEM((2, 2, 2, dp, 2, blocks, rows, 128), bf16),
+            pltpu.VMEM((dp, 2, groups, rows, 128), bf16),
             pltpu.VMEM((2, shard, 128), bf16),
             pltpu.VMEM((2, 2, blocks * 128, 128), bf16),
             pltpu.VMEM((2, 2, blocks * 128, 128), bf16),
@@ -286,20 +318,27 @@
         down_weight.reshape(dp, shard, 128),
         up_weight.reshape(dp, shard, 128),
     )
-    totals = totals.reshape(master.shape)
-    new_moment1 = 0.9 * moment1 + 0.1 * totals
-    new_moment2 = 0.95 * moment2 + 0.05 * totals * totals
-    first_fix = 1.0 - 0.9**STEP
-    second_fix = 1.0 - 0.95**STEP
-    new_master = master - 0.05 * (new_moment1 / first_fix) / (
-        jnp.sqrt(new_moment2 / second_fix) + 1e-08
-    )
+    state = totals.shape
+    results = pl.pallas_call(
+        adam_kernel,
+        out_shape=(
+            jax.ShapeDtypeStruct(down_values.shape, bf16),
+            jax.ShapeDtypeStruct(up_values.shape, bf16),
+            jax.ShapeDtypeStruct(state, f32),
+            jax.ShapeDtypeStruct(state, f32),
+            jax.ShapeDtypeStruct(state, f32),
+        ),
+        in_specs=[hbm, hbm, vmem, vmem, vmem, vmem],
+        out_specs=(hbm,) * 5,
+        scratch_shapes=[pltpu.VMEM((3,) + state, f32), DMA((2,)), DMA((3,) + state[:2])],
+        compiler_params=pltpu.CompilerParams(vmem_limit_bytes=8 * 1024 * 1024),
+    )(down_values, up_values, totals, master.reshape(state), moment1.reshape(state), moment2.reshape(state))
     return (
-        down_values.reshape(down_cot.shape),
-        up_values.reshape(up_cot.shape),
-        new_master,
-        new_moment1,
-        new_moment2,
+        results[0].reshape(down_cot.shape),
+        results[1].reshape(up_cot.shape),
+        results[2].reshape(master.shape),
+        results[3].reshape(master.shape),
+        results[4].reshape(master.shape),
     )
 
 

time: 57.4 us -> 54.2 us (0.944)
  other arithmetic: 2.37 us -> 0 us
  local copies, waits for them, and re-layouts: 1.35 us -> 0.01 us
  Pallas kernels: 52.8 us -> 53.4 us
    sub x1 -> x0, other arithmetic: 2.37 us -> none  [shards(): master - 0.05 * (new_moment1 / first_fix) / (jnp.sqrt(new_moment2 / secon...]
    unnamed x12 -> x6, local copies, waits for them, and re-layouts: 1.35 us -> 0.01 us
    pallas_call x1 -> x2, Pallas kernels: 52.8 us -> 53.4 us  [the longest x1 52 us: shards(): pl.pallas_call(relay_kernel, out_shape=(pltpu.VMEM((2, 2, blocks * 128, 1...]
where the time goes in v3:
time: 54.2 us; the launch traced here: 54.1 us
  Pallas kernels  53.4 us (99%)
  between operations  0.69 us (1%)
    pallas_call x1, Pallas kernels, shards(): pl.pallas_call(relay_kernel, out_shape=(pltpu.VMEM((2, 2, blocks * 128, 1...  52 us
    pallas_call x1, Pallas kernels, shards(): pl.pallas_call(adam_kernel, out_shape=(jax.ShapeDtypeStruct(down_values.s...  1.36 us

profile of v3, /device:TPU:1, one launch (start us, length us, event | category | flops | bytes accessed | tf_op | source)
XLA Modules:
  0.0 54.1 jit_solution(12124389593983832156)
XLA Ops:
  0.6 0.0 copy-start
  0.6 0.0 copy-start.1
  0.7 0.0 copy-start.2
  0.7 52.0 %shard_map.128 = (f32[2,2,256,128]{3,2,1,0:T(8,128)S(1)}, bf16[4,16,128]{2,1,0:T(8,128)(2,1)S(1)}, bf16[4,16,128]{2,1,0:T(8,128)(2,1)S(1)}) custom-call(bf16[4,16,4096]{2,1,0:T(8,128)(2,1)} %bitcast.19, bf16[4,16,4096]{2,1,0:T(8,128)(2,1)} %bitcast.20, bf16[4,16,128]{2,1,0:T(8,128)(2,1)} %bitcast.21, bf16[4,16,128]{2,1,0:T(8,128)(2,1)} %bitcast.22, ...), custom_call_target="tpu_custom_call" | custom-call | tf_op jit(solution)/shard_map/pallas_call | solution.py:277
  52.7 0.0 copy-done
  52.7 0.0 copy-done.1
  52.7 0.0 copy-done.2
  52.7 1.4 %shard_map.129 = (bf16[4,16,128]{2,1,0:T(8,128)(2,1)}, bf16[4,16,128]{2,1,0:T(8,128)(2,1)}, f32[2,2,256,128]{3,2,1,0:T(8,128)}, f32[2,2,256,128]{3,2,1,0:T(8,128)}, f32[2,2,256,128]{3,2,1,0:T(8,128)}) custom-call(bf16[4,16,128]{2,1,0:T(8,128)(2,1)S(1)} %get-tuple-element.13.down_values, bf16[4,16,128]{2,1,0:T(8,128)(2,1)S(1)} %get-tuple-element.14.up_values, ...), custom_call_target="tpu_custom_call" | custom-call | tf_op jit(solution)/shard_map/pallas_call | solution.py:322
Async XLA Ops:
  0.6 52.0 %copy-start = (f32[1,2,512,128]{3,2,1,0:T(8,128)S(1)}, f32[1,2,512,128]{3,2,1,0:T(8,128)}, u32[]{:S(2)}) copy-start(f32[1,2,512,128]{3,2,1,0:T(8,128)} %param.15) | copy-start | bytes 1572868
  0.6 52.0 %copy-start.1 = (f32[1,2,512,128]{3,2,1,0:T(8,128)S(1)}, f32[1,2,512,128]{3,2,1,0:T(8,128)}, u32[]{:S(2)}) copy-start(f32[1,2,512,128]{3,2,1,0:T(8,128)} %param.16) | copy-start | bytes 1572868
  0.7 52.0 %copy-start.2 = (f32[1,2,512,128]{3,2,1,0:T(8,128)S(1)}, f32[1,2,512,128]{3,2,1,0:T(8,128)}, u32[]{:S(2)}) copy-start(f32[1,2,512,128]{3,2,1,0:T(8,128)} %param.17) | copy-start | bytes 1572868

commit v4 on v3

--- a/solution.py
+++ b/solution.py
@@ -68,7 +68,8 @@
                     normed[way, peer, j, block] = (chosen * factor).astype(jnp.bfloat16)
 
     def relay(way):
-        for peer in range(dp):
+        for step in [(k + dp // 2) % dp for k in range(dp)]:
+            peer = lax.rem(d + step, dp)
             pltpu.make_async_remote_copy(
                 src_ref=normed.at[way, peer],
                 dst_ref=feats.at[way, half, pair, d],

time: 54.2 us -> 53.6 us (0.989)
  Pallas kernels: 53.4 us -> 52.5 us
    pallas_call x1, Pallas kernels: 52 us -> 51.1 us  [shards(): pl.pallas_call(relay_kernel, out_shape=(pltpu.VMEM((2, 2, blocks * 128, 1...]
where the time goes in v4:
time: 53.6 us; the launch traced here: 53.2 us
  Pallas kernels  52.5 us (98%)
  between operations  0.69 us (1%)
    pallas_call x1, Pallas kernels, shards(): pl.pallas_call(relay_kernel, out_shape=(pltpu.VMEM((2, 2, blocks * 128, 1...  51.1 us
    pallas_call x1, Pallas kernels, shards(): pl.pallas_call(adam_kernel, out_shape=(jax.ShapeDtypeStruct(down_values.s...  1.36 us

profile of v4, /device:TPU:1, one launch (start us, length us, event | category | flops | bytes accessed | tf_op | source)
XLA Modules:
  0.0 53.2 jit_solution(5085870809536205849)
XLA Ops:
  0.6 0.0 copy-start
  0.6 0.0 copy-start.1
  0.7 0.0 copy-start.2
  0.7 51.1 %shard_map.128 = (f32[2,2,256,128]{3,2,1,0:T(8,128)S(1)}, bf16[4,16,128]{2,1,0:T(8,128)(2,1)S(1)}, bf16[4,16,128]{2,1,0:T(8,128)(2,1)S(1)}) custom-call(bf16[4,16,4096]{2,1,0:T(8,128)(2,1)} %bitcast.19, bf16[4,16,4096]{2,1,0:T(8,128)(2,1)} %bitcast.20, bf16[4,16,128]{2,1,0:T(8,128)(2,1)} %bitcast.21, bf16[4,16,128]{2,1,0:T(8,128)(2,1)} %bitcast.22, ...), custom_call_target="tpu_custom_call" | custom-call | tf_op jit(solution)/shard_map/pallas_call | solution.py:278
  51.8 0.0 copy-done
  51.8 0.0 copy-done.1
  51.8 0.0 copy-done.2
  51.8 1.4 %shard_map.129 = (bf16[4,16,128]{2,1,0:T(8,128)(2,1)}, bf16[4,16,128]{2,1,0:T(8,128)(2,1)}, f32[2,2,256,128]{3,2,1,0:T(8,128)}, f32[2,2,256,128]{3,2,1,0:T(8,128)}, f32[2,2,256,128]{3,2,1,0:T(8,128)}) custom-call(bf16[4,16,128]{2,1,0:T(8,128)(2,1)S(1)} %get-tuple-element.13.down_values, bf16[4,16,128]{2,1,0:T(8,128)(2,1)S(1)} %get-tuple-element.14.up_values, ...), custom_call_target="tpu_custom_call" | custom-call | tf_op jit(solution)/shard_map/pallas_call | solution.py:323
Async XLA Ops:
  0.6 51.1 %copy-start = (f32[1,2,512,128]{3,2,1,0:T(8,128)S(1)}, f32[1,2,512,128]{3,2,1,0:T(8,128)}, u32[]{:S(2)}) copy-start(f32[1,2,512,128]{3,2,1,0:T(8,128)} %param.15) | copy-start | bytes 1572868
  0.6 51.1 %copy-start.1 = (f32[1,2,512,128]{3,2,1,0:T(8,128)S(1)}, f32[1,2,512,128]{3,2,1,0:T(8,128)}, u32[]{:S(2)}) copy-start(f32[1,2,512,128]{3,2,1,0:T(8,128)} %param.16) | copy-start | bytes 1572868
  0.7 51.1 %copy-start.2 = (f32[1,2,512,128]{3,2,1,0:T(8,128)S(1)}, f32[1,2,512,128]{3,2,1,0:T(8,128)}, u32[]{:S(2)}) copy-start(f32[1,2,512,128]{3,2,1,0:T(8,128)} %param.17) | copy-start | bytes 1572868
